TPU v7x, 32 devices: a whole 2x2x4 slice. The times are simulated.
32 devices in a mesh: gx: 8 (over z, x), gy: 4 (over y, core).
Axes of the slice: x: 2, y: 2, z: 4, core: 2. Of those that a mesh axis runs over, the one named last changes fastest.
Arguments:
- velocity: float32 [128, 3, 4, 16384], P('gx', None, None, 'gy'), may hold values from -6 to 6
- metric_x: float32 [128], P('gx'), may hold values from 0.5 to 2
- metric_y: float32 [16384], P('gy'), may hold values from 0.5 to 2
Outputs:
- deriv_x: float32 [128, 3, 4, 16384], P('gx', None, None, 'gy')
- deriv_y: float32 [128, 3, 4, 16384], P('gx', None, None, 'gy')
All inputs are finite; a program needn't handle non-finite values.
Results may differ from a plain program's by a relative error of at most 0.00007.
Values sent between devices are 32-bit elements; how exact they have to be, the bound alone decides.
A program may use at most 256 MiB of HBM per device.

v0:
```python
import functools
import math

import jax
import jax.numpy as jnp
import numpy as np
from jax import lax
from jax.experimental import pallas as pl
from jax.experimental.pallas import tpu as pltpu
from jax.sharding import PartitionSpec as P

ALPHA = 0.49
COEF = {1: 949.0 / 1200.0, 2: 167.0 / 1500.0, 3: -47.0 / 6000.0}
RATIO = (1.0 - math.sqrt(1.0 - 4.0 * ALPHA * ALPHA)) / (2.0 * ALPHA)
RHO = -RATIO
LEADING = 1.0 / (1.0 - 2.0 * ALPHA * RATIO)
MESH = pl.DeviceIdType.MESH
TILE = 128


def power(count):
    return float(RHO**count)


def response(offset):
    green = lambda n: LEADING * RHO ** abs(n)
    return sum(w * (green(offset - k) - green(offset + k)) for k, w in COEF.items())


WAVE = response(3) / RHO**2
BAND1 = response(1) - WAVE
BAND2 = response(2) - WAVE * RHO


def y_tables():
    own, up, down = (np.zeros((TILE, TILE)) for _ in range(3))
    for j in range(TILE):
        for l in range(TILE):
            own[j, l] = response(j - l)
            up[j, l] = response(j - TILE - l)
            down[j, l] = response(j + TILE - l)
    table = np.concatenate((own, up, down), 1)
    high = table.astype(jnp.bfloat16)
    low = (table - high.astype(np.float64)).astype(jnp.bfloat16)
    return np.concatenate((high, high, low), 0)


def edge_weights(cells):
    away = np.arange(cells, dtype=np.float64)
    return np.stack((RHO**away, RHO ** (cells - 1 - away))).astype(np.float32)


def exchange(nx, ny, v, wy, ein, halo, ygot, vbuf, esend, erecv, ssend, first, last, ysend,
             load_sem, edge_sem, own_sem, halo_send, halo_recv, e_s, e_r, s_s, s_r, y_s, y_r):
    cells, comps, planes, columns = v.shape
    width = columns // nx
    x, y = lax.axis_index("gx"), lax.axis_index("gy")

    def target(q):
        return lax.rem(x + 1 + q, nx)

    def load(q):
        at = pl.multiple_of(target(q) * width, TILE)
        return pltpu.make_async_copy(v.at[:, :, :, pl.ds(at, width)], vbuf.at[q % 2], load_sem.at[q % 2])

    load(0).start()
    edges = [
        pltpu.make_async_copy(v.at[:, :, :, pl.ds(0, TILE)], first, edge_sem.at[0]),
        pltpu.make_async_copy(v.at[:, :, :, pl.ds(columns - TILE, TILE)], last, edge_sem.at[1]),
    ]
    for copy in edges:
        copy.start()
    barrier = pltpu.get_barrier_semaphore()
    for q in range(nx - 1):
        pl.semaphore_signal(barrier, inc=1, device_id=(target(q), y), device_id_type=MESH)
    for q in range(ny - 1):
        pl.semaphore_signal(barrier, inc=1, device_id=(x, lax.rem(y + 1 + q, ny)), device_id_type=MESH)
    pl.semaphore_wait(barrier, nx + ny - 2)

    right, left = lax.rem(x + 1, nx), lax.rem(x + nx - 1, nx)
    rims = [
        pltpu.make_async_remote_copy(
            v.at[pl.ds(cells - 2, 2)], halo.at[0], halo_send.at[0], halo_recv.at[0],
            device_id=(right, y), device_id_type=MESH),
        pltpu.make_async_remote_copy(
            v.at[pl.ds(0, 2)], halo.at[1], halo_send.at[1], halo_recv.at[1],
            device_id=(left, y), device_id_type=MESH),
    ]
    for copy in rims:
        copy.start()

    sends = []
    to_low = jnp.zeros((cells, comps, planes, TILE), jnp.float32)
    to_high = jnp.zeros((cells, comps, planes, TILE), jnp.float32)
    ysum = [to_low, to_high]
    for q in range(nx):
        load(q).wait()
        if q + 1 < nx:
            load(q + 1).start()
        block = vbuf.at[q % 2]
        goes = esend.at[q] if q < nx - 1 else erecv.at[q]
        low, high = block[cells - 1], block[0]
        for i in range(1, cells):
            low = block[cells - 1 - i] + RHO * low
            high = block[i] + RHO * high
        goes[0] = low
        goes[1] = high
        if q < nx - 1:
            copy = pltpu.make_async_remote_copy(
                esend.at[q], erecv.at[q], e_s.at[q], e_r.at[q],
                device_id=(target(q), y), device_id_type=MESH)
            copy.start()
            sends.append(copy)
        start = target(q) * width
        for t in range(width // TILE):
            at = pl.multiple_of(start + t * TILE, TILE)
            part = block[:, :, :, t * TILE : (t + 1) * TILE]
            for side in range(2):
                ysum[side] = ysum[side] + part * wy[pl.ds(side, 1), pl.ds(at, TILE)][None, None]

    for copy in edges:
        copy.wait()
    lane = lax.broadcasted_iota(jnp.int32, (cells, comps, planes, TILE), 3)
    sums = [jnp.sum(part, axis=3, keepdims=True) for part in ysum]
    message = jnp.where(lane < 2, first[...], jnp.where(lane >= TILE - 2, last[...], 0.0))
    message = jnp.where(lane == 2, sums[0], jnp.where(lane == 3, sums[1], message))
    ysend[...] = message
    for q in range(ny - 1):
        copy = pltpu.make_async_remote_copy(
            ysend, ygot.at[q], y_s.at[q], y_r.at[q],
            device_id=(x, lax.rem(y + 1 + q, ny)), device_id_type=MESH)
        copy.start()
        sends.append(copy)
    own_y = pltpu.make_async_copy(ysend, ygot.at[ny - 1], own_sem.at[0])
    own_y.start()

    for copy in sends[: nx - 1]:
        copy.wait_recv()
    closing = 1.0 / (1.0 - power(cells * nx))
    spot = pl.multiple_of(x * width, TILE)
    for q in range(nx):
        from_low, from_high = 0.0, 0.0
        for s in range(nx):
            ahead = (q + s + 1) % nx + 1
            behind = (-(q + s + 2) - 1) % nx + 1
            from_low = from_low + closing * power(cells * (ahead - 1)) * erecv[s, 1]
            from_high = from_high + closing * power(cells * (behind - 1)) * erecv[s, 0]
        ssend[q, 0] = from_low
        ssend[q, 1] = from_high
        place = ein.at[:, :, :, pl.ds(spot, width)]
        if q < nx - 1:
            copy = pltpu.make_async_remote_copy(
                ssend.at[q], place, s_s.at[q], s_r.at[q],
                device_id=(target(q), y), device_id_type=MESH)
            copy.start()
            sends.append(copy)
        else:
            own_x = pltpu.make_async_copy(ssend.at[q], place, own_sem.at[1])
            own_x.start()
    own_y.wait()
    own_x.wait()
    for copy in rims:
        copy.wait()
    for copy in sends[: nx - 1]:
        copy.wait_send()
    for copy in sends[nx - 1 : nx + ny - 2]:
        copy.wait()
    for q, copy in enumerate(sends[nx + ny - 2 :]):
        copy.wait_send()
        at = pl.multiple_of(lax.rem(x + nx - 1 - q, nx) * width, TILE)
        pltpu.make_async_remote_copy(
            ssend.at[q], ein.at[:, :, :, pl.ds(at, width)], s_s.at[q], s_r.at[q],
            device_id=(target(q), y), device_id_type=MESH).wait_recv()


def derive(ny, mx, v, ein, halo, ygot, my, table, dx, dy, lhs, prod):
    cells, _, planes, columns = v.shape
    lines = cells * planes
    tiles = columns // TILE

    def flat(part):
        return part.reshape(lines, TILE)

    group = min(8, tiles)

    @pl.loop(0, tiles // group)
    def _(g):
        for t in range(group):
            at = pl.multiple_of((g * group + t) * TILE, TILE)
            part = flat(v[:, 0, :, pl.ds(at, TILE)])
            high = part.astype(jnp.bfloat16)
            low = (part - high.astype(jnp.float32)).astype(jnp.bfloat16)
            lhs[t * lines : (t + 1) * lines, 0:TILE] = high
            lhs[t * lines : (t + 1) * lines, TILE : 2 * TILE] = low
            lhs[t * lines : (t + 1) * lines, 2 * TILE :] = high
        rows = group * lines
        prod[pl.ds(pl.multiple_of(g * rows, rows), rows), :] = jnp.dot(
            lhs[...], table[...], preferred_element_type=jnp.float32)

    wide = 2 * TILE

    @pl.loop(0, columns // wide)
    def _(g):
        at = pl.ds(pl.multiple_of(g * wide, wide), wide)
        row = lambda i: (
            v[i, 0, :, at] if 0 <= i < cells
            else halo[0, 2 + i, 0, :, at] if i < 0
            else halo[1, i - cells, 0, :, at])
        above = [None] * cells
        above[cells - 1] = ein[1, 0, :, at]
        for i in range(cells - 1, 0, -1):
            above[i - 1] = row(i) + RHO * above[i]
        below = ein[0, 0, :, at]
        for i in range(cells):
            line = WAVE * (above[i] - below) + BAND1 * (row(i + 1) - row(i - 1))
            line = line + BAND2 * (row(i + 2) - row(i - 2))
            dx[i, 0, :, at] = mx[i] * line
            below = row(i) + RHO * below

    lane = lax.broadcasted_iota(jnp.int32, (1, TILE), 1)
    away = lane.astype(jnp.float32)
    sign = jnp.where(lane % 2 == 0, 1.0, -1.0).astype(jnp.float32)
    rise = WAVE * sign * jnp.exp(away * math.log(RATIO))
    fall = WAVE * -sign * jnp.exp((TILE - 1 - away) * math.log(RATIO))
    fall = -fall if TILE % 2 else fall
    step = power(columns)
    closing = 1.0 / (1.0 - power(columns * ny))
    low_in, high_in = 0.0, 0.0
    for s in range(ny):
        got = flat(ygot[s, :, 0])
        ahead = s + 1
        behind = ny - 1 - s if s < ny - 1 else ny
        low_in = low_in + closing * step ** (ahead - 1) * got[:, 3:4]
        high_in = high_in + closing * step ** (behind - 1) * got[:, 2:3]
    before = flat(ygot[0, :, 0])[:, TILE - 2 :]
    after = flat(ygot[ny - 2, :, 0])[:, 0:2]
    jump = power(TILE)

    def at_lane(n, value):
        return jnp.where(lane == n, value, 0.0)

    highs = [None] * tiles
    far = high_in
    for k in range(tiles - 1, -1, -1):
        highs[k] = far
        if k:
            seen = prod[k * lines : (k + 1) * lines, 3 * TILE - 3 : 3 * TILE - 2]
            far = seen * (1.0 / (WAVE * RHO**2)) + jump * far
    far = low_in
    for k in range(tiles):
        rows = slice(k * lines, (k + 1) * lines)
        line = prod[rows, 0:TILE]
        if k:
            line = line + prod[(k - 1) * lines : k * lines, TILE : 2 * TILE]
            line = line - (jump * past) * rise
        else:
            line = line - far * rise
            line = line - at_lane(0, BAND1 * before[:, 1:2] + BAND2 * before[:, 0:1])
            line = line - at_lane(1, BAND2 * before[:, 1:2])
        if k < tiles - 1:
            line = line + prod[(k + 1) * lines : (k + 2) * lines, 2 * TILE :]
            line = line + (jump * highs[k + 1]) * fall
        else:
            line = line + highs[k] * fall
            line = line + at_lane(TILE - 1, BAND1 * after[:, 0:1] + BAND2 * after[:, 1:2])
            line = line + at_lane(TILE - 2, BAND2 * after[:, 0:1])
        at = slice(k * TILE, (k + 1) * TILE)
        dy[:, 0, :, at] = (line * my[:, at]).reshape(cells, planes, TILE)
        past = far
        seen = prod[rows, TILE + 2 : TILE + 3]
        far = seen * (-1.0 / (WAVE * RHO**2)) + jump * past


def body(nx, ny, velocity, metric_x, metric_y):
    cells, comps, planes, columns = velocity.shape
    width = columns // nx
    f32 = jnp.float32
    dma = pltpu.SemaphoreType.DMA
    hbm = pl.BlockSpec(memory_space=pl.ANY)
    ein, halo, ygot = pl.pallas_call(
        functools.partial(exchange, nx, ny),
        out_shape=[
            jax.ShapeDtypeStruct((2, comps, planes, columns), f32),
            jax.ShapeDtypeStruct((2, 2, comps, planes, columns), f32),
            jax.ShapeDtypeStruct((ny, cells, comps, planes, TILE), f32),
        ],
        in_specs=[hbm, pl.BlockSpec(memory_space=pltpu.VMEM)],
        out_specs=[hbm, hbm, hbm],
        scratch_shapes=[
            pltpu.VMEM((2, cells, comps, planes, width), f32),
            pltpu.VMEM((nx, 2, comps, planes, width), f32),
            pltpu.VMEM((nx, 2, comps, planes, width), f32),
            pltpu.VMEM((nx, 2, comps, planes, width), f32),
            pltpu.VMEM((cells, comps, planes, TILE), f32),
            pltpu.VMEM((cells, comps, planes, TILE), f32),
            pltpu.VMEM((cells, comps, planes, TILE), f32),
            dma((2,)), dma((2,)), dma((2,)), dma((2,)), dma((2,)),
            dma((nx,)), dma((nx,)), dma((nx,)), dma((nx,)), dma((ny,)), dma((ny,)),
        ],
        compiler_params=pltpu.CompilerParams(
            collective_id=0, has_side_effects=True, vmem_limit_bytes=32 * 2**20),
        name="exchange",
    )(velocity, edge_weights(columns))

    lines = cells * planes
    tiles = columns // TILE
    plane = pl.BlockSpec((cells, 1, planes, columns), lambda c: (0, c, 0, 0))
    deriv_x, deriv_y = pl.pallas_call(
        functools.partial(derive, ny),
        grid=(comps,),
        out_shape=[jax.ShapeDtypeStruct(velocity.shape, f32)] * 2,
        in_specs=[
            pl.BlockSpec(memory_space=pltpu.SMEM),
            plane,
            pl.BlockSpec((2, 1, planes, columns), lambda c: (0, c, 0, 0)),
            pl.BlockSpec((2, 2, 1, planes, columns), lambda c: (0, 0, c, 0, 0)),
            pl.BlockSpec((ny, cells, 1, planes, TILE), lambda c: (0, 0, c, 0, 0)),
            pl.BlockSpec((1, columns), lambda c: (0, 0)),
            pl.BlockSpec((3 * TILE, 3 * TILE), lambda c: (0, 0)),
        ],
        out_specs=[plane, plane],
        scratch_shapes=[
            pltpu.VMEM((min(8, tiles) * lines, 3 * TILE), jnp.bfloat16),
            pltpu.VMEM((tiles * lines, 3 * TILE), f32),
        ],
        compiler_params=pltpu.CompilerParams(vmem_limit_bytes=40 * 2**20),
        name="derive",
    )(metric_x, velocity, ein, halo, ygot, metric_y[None, :], y_tables())
    return deriv_x, deriv_y


def solution(mesh):
    placed = (P("gx", None, None, "gy"), P("gx"), P("gy"))
    return jax.shard_map(
        functools.partial(body, mesh.shape["gx"], mesh.shape["gy"]),
        mesh=mesh,
        in_specs=placed,
        out_specs=(P("gx", None, None, "gy"), P("gx", None, None, "gy")),
        check_vma=False,
    )
```

profile of v0, /device:TPU:0, one launch (start us, length us, event | category | flops | bytes accessed | tf_op | source)
XLA Modules:
  0.0 53.2 jit_solution(12681043818610151706)
XLA Ops:
  0.6 0.0 copy-start.5
  0.6 0.0 copy-start
  0.6 1.9 %copy-done = f32[16,3,4,4096]{3,2,1,0:T(4,128)S(1)} copy-done((f32[16,3,4,4096]{3,2,1,0:T(4,128)S(1)}, f32[16,3,4,4096]{3,2,1,0:T(4,128)}, u32[]{:S(2)}) %copy-start) | copy-done | bytes 3145752
  2.5 0.0 copy-start.3
  2.5 0.8 %copy-done.3 = f32[2,4096]{1,0:T(2,128)S(1)} copy-done((f32[2,4096]{1,0:T(2,128)S(1)}, f32[2,4096]{1,0:T(2,128)}, u32[]{:S(2)}) %copy-start.3) | copy-done | bytes 32792
  3.3 0.0 copy-start.1
  3.3 0.0 copy-start.4
  3.3 36.7 %exchange.1 = (f32[2,3,4,4096]{3,2,1,0:T(4,128)S(1)}, f32[2,2,3,4,4096]{4,3,2,1,0:T(4,128)S(1)}, f32[4,16,3,4,128]{4,3,2,1,0:T(4,128)S(1)}) custom-call(f32[16,3,4,4096]{3,2,1,0:T(4,128)S(1)} %copy-done, f32[2,4096]{1,0:T(2,128)S(1)} %copy-done.3), custom_call_target="tpu_custom_call" | custom-call | tf_op jit(solution)/shard_map/exchange/pallas_call | solution.py:280
  40.0 0.0 copy-done.5
  40.0 0.0 copy-done.1
  40.0 0.0 copy-done.4
  40.0 0.0 copy-start.2
  40.0 1.0 %copy-done.2 = bf16[384,384]{1,0:T(8,128)(2,1)S(1)} copy-done((bf16[384,384]{1,0:T(8,128)(2,1)S(1)}, bf16[384,384]{1,0:T(8,128)(2,1)}, u32[]{:S(2)}) %copy-start.2) | copy-done | bytes 294936
  41.0 12.3 %derive.1 = (f32[16,3,4,4096]{3,2,1,0:T(4,128)}, f32[16,3,4,4096]{3,2,1,0:T(4,128)}) custom-call(f32[16]{0:T(128)S(1)} %copy-done.5, f32[16,3,4,4096]{3,2,1,0:T(4,128)S(1)} %copy-done.1, f32[2,3,4,4096]{3,2,1,0:T(4,128)S(1)} %get-tuple-element.5.ein, f32[2,2,3,4,4096]{4,3,2,1,0:T(4,128)S(1)} %get-tuple-element.6.halo, ...), custom_call_target="tpu_custom_call" | custom-call | tf_op jit(solution)/shard_map/derive/pallas_call | solution.py:308
Async XLA Ops:
  0.6 39.3 %copy-start.5 = (f32[16]{0:T(128)S(1)}, f32[16]{0:T(128)}, u32[]{:S(2)}) copy-start(f32[16]{0:T(128)} %mx.1) | copy-start | bytes 196
  0.6 1.9 %copy-start = (f32[16,3,4,4096]{3,2,1,0:T(4,128)S(1)}, f32[16,3,4,4096]{3,2,1,0:T(4,128)}, u32[]{:S(2)}) copy-start(f32[16,3,4,4096]{3,2,1,0:T(4,128)} %v.3) | copy-start | bytes 9437188
  2.5 0.8 %copy-start.3 = (f32[2,4096]{1,0:T(2,128)S(1)}, f32[2,4096]{1,0:T(2,128)}, u32[]{:S(2)}) copy-start(f32[2,4096]{1,0:T(2,128)} %constant.4.clone.wy) | copy-start | bytes 98308
  3.3 36.7 %copy-start.1 = (f32[16,3,4,4096]{3,2,1,0:T(4,128)S(1)}, f32[16,3,4,4096]{3,2,1,0:T(4,128)}, u32[]{:S(2)}) copy-start(f32[16,3,4,4096]{3,2,1,0:T(4,128)} %v.3) | copy-start | bytes 9437188
  3.3 36.7 %copy-start.4 = (f32[4096]{0:T(1024)S(1)}, f32[4096]{0:T(1024)}, u32[]{:S(2)}) copy-start(f32[4096]{0:T(1024)} %param.7) | copy-start | bytes 49156
  40.0 1.0 %copy-start.2 = (bf16[384,384]{1,0:T(8,128)(2,1)S(1)}, bf16[384,384]{1,0:T(8,128)(2,1)}, u32[]{:S(2)}) copy-start(bf16[384,384]{1,0:T(8,128)(2,1)} %constant.5.clone.table) | copy-start | bytes 884740
where the time goes:
time: 53.5 us; the launch traced here: 53.2 us
  Pallas kernels  48.9 us (91%)
  local copies, waits for them, and re-layouts  3.61 us (7%)
  between operations  0.69 us (1%)
    pallas_call x1, Pallas kernels, body(): pl.pallas_call(functools.partial(exchange, nx, ny), out_shape=[jax.ShapeD...  36.7 us
    pallas_call x1, Pallas kernels, body(): pl.pallas_call(functools.partial(derive, ny), grid=(comps,), out_shape=[j...  12.3 us
    unnamed x12, local copies, waits for them, and re-layouts  3.61 us

commit v1 on v0

--- a/solution.py
+++ b/solution.py
@@ -16,6 +16,7 @@
 LEADING = 1.0 / (1.0 - 2.0 * ALPHA * RATIO)
 MESH = pl.DeviceIdType.MESH
 TILE = 128
+PARTS = 2
 
 
 def power(count):
@@ -45,13 +46,13 @@
     return np.concatenate((high, high, low), 0)
 
 
-def edge_weights(cells):
-    away = np.arange(cells, dtype=np.float64)
-    return np.stack((RHO**away, RHO ** (cells - 1 - away))).astype(np.float32)
-
-
-def exchange(nx, ny, v, wy, ein, halo, ygot, vbuf, esend, erecv, ssend, first, last, ysend,
-             load_sem, edge_sem, own_sem, halo_send, halo_recv, e_s, e_r, s_s, s_r, y_s, y_r):
+def signed_power(count):
+    size = jnp.exp(count.astype(jnp.float32) * math.log(RATIO))
+    return jnp.where(count % 2 == 0, size, -size)
+
+
+def exchange(nx, ny, v, ein, ygot, vbuf, esend, erecv, ssend, first, last, ysend,
+             load_sem, edge_sem, own_sem, e_s, e_r, s_s, s_r, y_s, y_r):
     cells, comps, planes, columns = v.shape
     width = columns // nx
     x, y = lax.axis_index("gx"), lax.axis_index("gy")
@@ -76,18 +77,6 @@
     for q in range(ny - 1):
         pl.semaphore_signal(barrier, inc=1, device_id=(x, lax.rem(y + 1 + q, ny)), device_id_type=MESH)
     pl.semaphore_wait(barrier, nx + ny - 2)
-
-    right, left = lax.rem(x + 1, nx), lax.rem(x + nx - 1, nx)
-    rims = [
-        pltpu.make_async_remote_copy(
-            v.at[pl.ds(cells - 2, 2)], halo.at[0], halo_send.at[0], halo_recv.at[0],
-            device_id=(right, y), device_id_type=MESH),
-        pltpu.make_async_remote_copy(
-            v.at[pl.ds(0, 2)], halo.at[1], halo_send.at[1], halo_recv.at[1],
-            device_id=(left, y), device_id_type=MESH),
-    ]
-    for copy in rims:
-        copy.start()
 
     sends = []
     to_low = jnp.zeros((cells, comps, planes, TILE), jnp.float32)
@@ -113,10 +102,11 @@
             sends.append(copy)
         start = target(q) * width
         for t in range(width // TILE):
-            at = pl.multiple_of(start + t * TILE, TILE)
+            at = start + t * TILE
             part = block[:, :, :, t * TILE : (t + 1) * TILE]
-            for side in range(2):
-                ysum[side] = ysum[side] + part * wy[pl.ds(side, 1), pl.ds(at, TILE)][None, None]
+            cell = at + lax.broadcasted_iota(jnp.int32, (1, 1, 1, TILE), 3)
+            for side, away in enumerate((cell, columns - 1 - cell)):
+                ysum[side] = ysum[side] + part * signed_power(away)
 
     for copy in edges:
         copy.wait()
@@ -159,8 +149,6 @@
             own_x.start()
     own_y.wait()
     own_x.wait()
-    for copy in rims:
-        copy.wait()
     for copy in sends[: nx - 1]:
         copy.wait_send()
     for copy in sends[nx - 1 : nx + ny - 2]:
@@ -173,7 +161,30 @@
             device_id=(target(q), y), device_id_type=MESH).wait_recv()
 
 
-def derive(ny, mx, v, ein, halo, ygot, my, table, dx, dy, lhs, prod):
+def derive_x(mx, v, ein, low, high, *rest):
+    dx = rest[-1]
+    cells, _, planes, columns = v.shape
+    wide = 2 * TILE
+
+    @pl.loop(0, columns // wide)
+    def _(g):
+        at = pl.ds(pl.multiple_of(g * wide, wide), wide)
+        row = lambda i: (
+            v[i, 0, :, at] if 0 <= i < cells
+            else low[2 + i, 0, :, at] if i < 0
+            else high[i - cells, 0, :, at])
+        above = [None] * cells
+        above[cells - 1] = ein[1, 0, :, at]
+        for i in range(cells - 1, 0, -1):
+            above[i - 1] = row(i) + RHO * above[i]
+        below = ein[0, 0, :, at]
+        for i in range(cells):
+            line = WAVE * (above[i] - below) + BAND1 * (row(i + 1) - row(i - 1))
+            line = line + BAND2 * (row(i + 2) - row(i - 2))
+            dx[i, 0, :, at] = mx[i] * line
+            below = row(i) + RHO * below
+
+def derive_y(ny, v, ygot, my, table, dy, lhs, prod):
     cells, _, planes, columns = v.shape
     lines = cells * planes
     tiles = columns // TILE
@@ -196,26 +207,6 @@
         rows = group * lines
         prod[pl.ds(pl.multiple_of(g * rows, rows), rows), :] = jnp.dot(
             lhs[...], table[...], preferred_element_type=jnp.float32)
-
-    wide = 2 * TILE
-
-    @pl.loop(0, columns // wide)
-    def _(g):
-        at = pl.ds(pl.multiple_of(g * wide, wide), wide)
-        row = lambda i: (
-            v[i, 0, :, at] if 0 <= i < cells
-            else halo[0, 2 + i, 0, :, at] if i < 0
-            else halo[1, i - cells, 0, :, at])
-        above = [None] * cells
-        above[cells - 1] = ein[1, 0, :, at]
-        for i in range(cells - 1, 0, -1):
-            above[i - 1] = row(i) + RHO * above[i]
-        below = ein[0, 0, :, at]
-        for i in range(cells):
-            line = WAVE * (above[i] - below) + BAND1 * (row(i + 1) - row(i - 1))
-            line = line + BAND2 * (row(i + 2) - row(i - 2))
-            dx[i, 0, :, at] = mx[i] * line
-            below = row(i) + RHO * below
 
     lane = lax.broadcasted_iota(jnp.int32, (1, TILE), 1)
     away = lane.astype(jnp.float32)
@@ -274,18 +265,24 @@
 def body(nx, ny, velocity, metric_x, metric_y):
     cells, comps, planes, columns = velocity.shape
     width = columns // nx
+    part = columns // PARTS
     f32 = jnp.float32
     dma = pltpu.SemaphoreType.DMA
     hbm = pl.BlockSpec(memory_space=pl.ANY)
-    ein, halo, ygot = pl.pallas_call(
+    up = [(i, (i + 1) % nx) for i in range(nx)]
+    down = [(i, (i - 1) % nx) for i in range(nx)]
+    rims = []
+    for p in range(PARTS):
+        here = velocity[:, :, :, p * part : (p + 1) * part]
+        rims.append((lax.ppermute(here[cells - 2 :], "gx", up), lax.ppermute(here[:2], "gx", down)))
+    ein, ygot = pl.pallas_call(
         functools.partial(exchange, nx, ny),
         out_shape=[
             jax.ShapeDtypeStruct((2, comps, planes, columns), f32),
-            jax.ShapeDtypeStruct((2, 2, comps, planes, columns), f32),
             jax.ShapeDtypeStruct((ny, cells, comps, planes, TILE), f32),
         ],
-        in_specs=[hbm, pl.BlockSpec(memory_space=pltpu.VMEM)],
-        out_specs=[hbm, hbm, hbm],
+        in_specs=[hbm],
+        out_specs=[hbm, hbm],
         scratch_shapes=[
             pltpu.VMEM((2, cells, comps, planes, width), f32),
             pltpu.VMEM((nx, 2, comps, planes, width), f32),
@@ -294,38 +291,68 @@
             pltpu.VMEM((cells, comps, planes, TILE), f32),
             pltpu.VMEM((cells, comps, planes, TILE), f32),
             pltpu.VMEM((cells, comps, planes, TILE), f32),
-            dma((2,)), dma((2,)), dma((2,)), dma((2,)), dma((2,)),
+            dma((2,)), dma((2,)), dma((2,)),
             dma((nx,)), dma((nx,)), dma((nx,)), dma((nx,)), dma((ny,)), dma((ny,)),
         ],
         compiler_params=pltpu.CompilerParams(
             collective_id=0, has_side_effects=True, vmem_limit_bytes=32 * 2**20),
+        cost_estimate=pl.CostEstimate(
+            flops=8 * velocity.size, bytes_accessed=4 * velocity.size, transcendentals=0),
         name="exchange",
-    )(velocity, edge_weights(columns))
+    )(velocity)
 
     lines = cells * planes
     tiles = columns // TILE
+    both = pl.CostEstimate(
+        flops=20 * velocity.size, bytes_accessed=8 * velocity.size, transcendentals=0)
     plane = pl.BlockSpec((cells, 1, planes, columns), lambda c: (0, c, 0, 0))
-    deriv_x, deriv_y = pl.pallas_call(
-        functools.partial(derive, ny),
+    deriv_y = pl.pallas_call(
+        functools.partial(derive_y, ny),
         grid=(comps,),
-        out_shape=[jax.ShapeDtypeStruct(velocity.shape, f32)] * 2,
+        out_shape=jax.ShapeDtypeStruct(velocity.shape, f32),
         in_specs=[
-            pl.BlockSpec(memory_space=pltpu.SMEM),
             plane,
-            pl.BlockSpec((2, 1, planes, columns), lambda c: (0, c, 0, 0)),
-            pl.BlockSpec((2, 2, 1, planes, columns), lambda c: (0, 0, c, 0, 0)),
             pl.BlockSpec((ny, cells, 1, planes, TILE), lambda c: (0, 0, c, 0, 0)),
             pl.BlockSpec((1, columns), lambda c: (0, 0)),
             pl.BlockSpec((3 * TILE, 3 * TILE), lambda c: (0, 0)),
         ],
-        out_specs=[plane, plane],
+        out_specs=plane,
         scratch_shapes=[
             pltpu.VMEM((min(8, tiles) * lines, 3 * TILE), jnp.bfloat16),
             pltpu.VMEM((tiles * lines, 3 * TILE), f32),
         ],
-        compiler_params=pltpu.CompilerParams(vmem_limit_bytes=40 * 2**20),
-        name="derive",
-    )(metric_x, velocity, ein, halo, ygot, metric_y[None, :], y_tables())
+        compiler_params=pltpu.CompilerParams(vmem_limit_bytes=32 * 2**20),
+        cost_estimate=both,
+        name="derive_y",
+    )(velocity, ygot, metric_y[None, :], y_tables())
+
+    deriv_x = None
+    for p in range(PARTS):
+        spread = lambda c, p=p: (0, c, 0, p)
+        whole = lambda c: (0, c, 0, 0)
+        operands = [metric_x, velocity, ein, *rims[p]]
+        specs = [
+            pl.BlockSpec(memory_space=pltpu.SMEM),
+            pl.BlockSpec((cells, 1, planes, part), spread),
+            pl.BlockSpec((2, 1, planes, part), spread),
+            pl.BlockSpec((2, 1, planes, part), whole),
+            pl.BlockSpec((2, 1, planes, part), whole),
+        ]
+        if p:
+            operands.append(deriv_x)
+            specs.append(hbm)
+        deriv_x = pl.pallas_call(
+            derive_x,
+            grid=(comps,),
+            out_shape=jax.ShapeDtypeStruct(velocity.shape, f32),
+            in_specs=specs,
+            out_specs=pl.BlockSpec((cells, 1, planes, part), spread),
+            input_output_aliases={5: 0} if p else {},
+            compiler_params=pltpu.CompilerParams(vmem_limit_bytes=24 * 2**20),
+            cost_estimate=pl.CostEstimate(
+                flops=both.flops // PARTS, bytes_accessed=both.bytes_accessed // PARTS, transcendentals=0),
+            name=f"derive_x{p}",
+        )(*operands)
     return deriv_x, deriv_y
 
 

time: 53.5 us -> 53.2 us (level)
  starting transfers between devices: 0 us -> 10.8 us
  Pallas kernels: 48.9 us -> 38.2 us
    pallas_call x1, Pallas kernels: 36.7 us -> 23.1 us  [body(): pl.pallas_call(functools.partial(exchange, nx, ny), out_shape=[jax.ShapeD...]
    ppermute x0 -> x4, starting transfers between devices: none -> 10.8 us  [the longest x2 7.82 us: body(): lax.ppermute(here[:2], 'gx', down)]
    pallas_call x1 -> x3, Pallas kernels: 12.3 us -> 15.1 us  [the longest x1 9.33 us: body(): pl.pallas_call(functools.partial(derive_y, ny), grid=(comps,), out_shape=...]
    unnamed x12 -> x8, local copies, waits for them, and re-layouts: 3.61 us -> 1.91 us
    slice x0 -> x1, local copies, waits for them, and re-layouts: none -> 1.32 us  [body(): here[:2]]
  transfers between devices with their start and end apart: 0 -> 4, of which waited for: 0 -> 0; matrix products, arithmetic and copies ran while one was open for 0% -> 0% of each run, Pallas kernels for 0% -> 67%
where the time goes in v1:
time: 53.2 us; the launch traced here: 53 us
  Pallas kernels  38.2 us (72%)
  starting transfers between devices  10.8 us (20%)
  local copies, waits for them, and re-layouts  3.23 us (6%)
  between operations  0.69 us (1%)
    pallas_call x1, Pallas kernels, body(): pl.pallas_call(functools.partial(exchange, nx, ny), out_shape=[jax.ShapeD...  23.1 us
    pallas_call x1, Pallas kernels, body(): pl.pallas_call(functools.partial(derive_y, ny), grid=(comps,), out_shape=...  9.33 us
    ppermute x2, starting transfers between devices, body(): lax.ppermute(here[:2], 'gx', down)  7.82 us
    pallas_call x2, Pallas kernels, body(): pl.pallas_call(derive_x, grid=(comps,), out_shape=jax.ShapeDtypeStruct(ve...  5.8 us
    ppermute x2, starting transfers between devices, body(): lax.ppermute(here[cells - 2:], 'gx', up)  2.99 us
    unnamed x8, local copies, waits for them, and re-layouts  1.91 us
    slice x1, local copies, waits for them, and re-layouts, body(): here[:2]  1.32 us
  transfers between devices with their start and end apart: 4, of which 0 were waited for; matrix products, arithmetic and copies ran while one was open for 0% of the time, Pallas kernels for 67%

profile of v1, /device:TPU:0, one launch (start us, length us, event | category | flops | bytes accessed | tf_op | source)
XLA Modules:
  0.0 53.0 jit_solution(10744207757353810880)
XLA Ops:
  0.6 0.0 copy-start.1
  0.6 0.0 copy-start.2
  0.7 1.3 %fusion = (f32[2,3,4,2048]{3,2,1,0:T(4,128)S(1)}, f32[2,3,4,2048]{3,2,1,0:T(4,128)S(1)}, f32[2,3,4,2048]{3,2,1,0:T(4,128)S(1)}, f32[2,3,4,2048]{3,2,1,0:T(4,128)S(1)}) fusion(f32[16,3,4,4096]{3,2,1,0:T(4,128)} %v.7), kind=kLoop, calls=%fused_computation | loop fusion | bytes 1572864 | tf_op jit(solution)/shard_map/slice | solution.py:277
  2.0 3.0 %collective-permute-start.2 = (f32[2,3,4,2048]{3,2,1,0:T(4,128)S(1)}, f32[2,3,4,2048]{3,2,1,0:T(4,128)S(1)}, u32[]{:S(2)}, u32[]{:S(2)}) collective-permute-start(f32[2,3,4,2048]{3,2,1,0:T(4,128)S(1)} %get-tuple-element.7), channel_id=1, source_target_pairs={{0,4},{4,8},{8,12},{12,16},{16,20},{20,24},{24,28},{28,0},{1,5},{5... | collective-permute-start | bytes 589832 | tf_op jit(solution)/shard_map/ppermute | solution.py:277
  5.0 3.1 %collective-permute-start.3 = (f32[2,3,4,2048]{3,2,1,0:T(4,128)S(1)}, f32[2,3,4,2048]{3,2,1,0:T(4,128)S(1)}, u32[]{:S(2)}, u32[]{:S(2)}) collective-permute-start(f32[2,3,4,2048]{3,2,1,0:T(4,128)S(1)} %get-tuple-element.6), channel_id=1, source_target_pairs={{0,28},{4,0},{8,4},{12,8},{16,12},{20,16},{24,20},{28,24},{1,29},{... | collective-permute-start | bytes 589832 | tf_op jit(solution)/shard_map/ppermute | solution.py:277
  8.1 0.0 collective-permute-start
  8.1 4.7 %collective-permute-start.1 = (f32[2,3,4,2048]{3,2,1,0:T(4,128)S(1)}, f32[2,3,4,2048]{3,2,1,0:T(4,128)S(1)}, u32[]{:S(2)}, u32[]{:S(2)}) collective-permute-start(f32[2,3,4,2048]{3,2,1,0:T(4,128)S(1)} %get-tuple-element.8), channel_id=1, source_target_pairs={{0,28},{4,0},{8,4},{12,8},{16,12},{20,16},{24,20},{28,24},{1,29},{... | collective-permute-start | bytes 589832 | tf_op jit(solution)/shard_map/ppermute | solution.py:277
  12.8 0.0 copy-start
  12.8 1.9 %copy-done = f32[16,3,4,4096]{3,2,1,0:T(4,128)S(1)} copy-done((f32[16,3,4,4096]{3,2,1,0:T(4,128)S(1)}, f32[16,3,4,4096]{3,2,1,0:T(4,128)}, u32[]{:S(2)}) %copy-start) | copy-done | bytes 3145752
  14.7 23.1 %exchange.1 = (f32[2,3,4,4096]{3,2,1,0:T(4,128)S(1)}, f32[4,16,3,4,128]{4,3,2,1,0:T(4,128)S(1)}) custom-call(f32[16,3,4,4096]{3,2,1,0:T(4,128)S(1)} %copy-done), custom_call_target="tpu_custom_call" | custom-call | flops 6291456 | bytes 3145728 | tf_op jit(solution)/shard_map/exchange/pallas_call | solution.py:278
  37.8 0.0 copy-done.1
  37.8 0.0 copy-done.2
  37.8 0.0 copy-start.3
  37.8 9.3 %derive_y.1 = f32[16,3,4,4096]{3,2,1,0:T(4,128)} custom-call(f32[16,3,4,4096]{3,2,1,0:T(4,128)S(1)} %copy-done, f32[4,16,3,4,128]{4,3,2,1,0:T(4,128)S(1)} %get-tuple-element.5.ygot, f32[1,4096]{1,0:T(1,128)S(1)} %bitcast.1, bf16[384,384]{1,0:T(8,128)(2,1)S(1)} %copy-done.1), custom_call_target="tpu_custom_call" | custom-call | flops 15728640 | bytes 6291456 | tf_op jit(solution)/shard_map/derive_y/pallas_call | solution.py:309
  47.2 0.0 collective-permute-done.2.low
  47.2 0.0 collective-permute-done.3.high
  47.2 0.0 copy-done.3
  47.2 2.9 %derive_x0.1.rest_0_ = f32[16,3,4,4096]{3,2,1,0:T(4,128)} custom-call(f32[16]{0:T(128)S(1)} %copy-done.3, f32[16,3,4,4096]{3,2,1,0:T(4,128)S(1)} %copy-done, f32[2,3,4,4096]{3,2,1,0:T(4,128)S(1)} %get-tuple-element.4.ein, f32[2,3,4,2048]{3,2,1,0:T(4,128)S(1)} %collective-permute-done.2.low, f32[2,3,4,2048]{3,2,1,0:T(4,128)S(1)} %collective-permute-done.3.high), custom_call_target="tpu_custom_call" | custom-call | flops 7864320 | bytes 3145728 | tf_op jit(solution)/shard_map/derive_x0/pallas_call | solution.py:344
  50.1 0.0 collective-permute-done.low
  50.1 0.0 collective-permute-done.1.high
  50.1 2.9 %derive_x1.1 = f32[16,3,4,4096]{3,2,1,0:T(4,128)} custom-call(f32[16]{0:T(128)S(1)} %copy-done.3, f32[16,3,4,4096]{3,2,1,0:T(4,128)S(1)} %copy-done, f32[2,3,4,4096]{3,2,1,0:T(4,128)S(1)} %get-tuple-element.4.ein, f32[2,3,4,2048]{3,2,1,0:T(4,128)S(1)} %collective-permute-done.low, ...), custom_call_target="tpu_custom_call", output_to_operand_aliasing={{}: (5, {})} | custom-call | flops 7864320 | bytes 3145728 | tf_op jit(solution)/shard_map/derive_x1/pallas_call | solution.py:344
Async XLA Ops:
  0.6 37.2 %copy-start.1 = (bf16[384,384]{1,0:T(8,128)(2,1)S(1)}, bf16[384,384]{1,0:T(8,128)(2,1)}, u32[]{:S(2)}) copy-start(bf16[384,384]{1,0:T(8,128)(2,1)} %constant.2.clone.table) | copy-start | bytes 884740
  0.6 37.2 %copy-start.2 = (f32[4096]{0:T(1024)S(1)}, f32[4096]{0:T(1024)}, u32[]{:S(2)}) copy-start(f32[4096]{0:T(1024)} %param.6) | copy-start | bytes 49156
  2.0 45.2 %collective-permute-start.2 = (f32[2,3,4,2048]{3,2,1,0:T(4,128)S(1)}, f32[2,3,4,2048]{3,2,1,0:T(4,128)S(1)}, u32[]{:S(2)}, u32[]{:S(2)}) collective-permute-start(f32[2,3,4,2048]{3,2,1,0:T(4,128)S(1)} %get-tuple-element.7), channel_id=1, source_target_pairs={{0,4},{4,8},{8,12},{12,16},{16,20},{20,24},{24,28},{28,0},{1,5},{5... | collective-permute-start | bytes 589832 | tf_op jit(solution)/shard_map/ppermute | solution.py:277
  5.0 42.2 %collective-permute-start.3 = (f32[2,3,4,2048]{3,2,1,0:T(4,128)S(1)}, f32[2,3,4,2048]{3,2,1,0:T(4,128)S(1)}, u32[]{:S(2)}, u32[]{:S(2)}) collective-permute-start(f32[2,3,4,2048]{3,2,1,0:T(4,128)S(1)} %get-tuple-element.6), channel_id=1, source_target_pairs={{0,28},{4,0},{8,4},{12,8},{16,12},{20,16},{24,20},{28,24},{1,29},{... | collective-permute-start | bytes 589832 | tf_op jit(solution)/shard_map/ppermute | solution.py:277
  8.1 42.0 %collective-permute-start = (f32[2,3,4,2048]{3,2,1,0:T(4,128)S(1)}, f32[2,3,4,2048]{3,2,1,0:T(4,128)S(1)}, u32[]{:S(2)}, u32[]{:S(2)}) collective-permute-start(f32[2,3,4,2048]{3,2,1,0:T(4,128)S(1)} %get-tuple-element.9), channel_id=1, source_target_pairs={{0,4},{4,8},{8,12},{12,16},{16,20},{20,24},{24,28},{28,0},{1,5},{5... | collective-permute-start | bytes 589832 | tf_op jit(solution)/shard_map/ppermute | solution.py:277
  8.1 42.0 %collective-permute-start.1 = (f32[2,3,4,2048]{3,2,1,0:T(4,128)S(1)}, f32[2,3,4,2048]{3,2,1,0:T(4,128)S(1)}, u32[]{:S(2)}, u32[]{:S(2)}) collective-permute-start(f32[2,3,4,2048]{3,2,1,0:T(4,128)S(1)} %get-tuple-element.8), channel_id=1, source_target_pairs={{0,28},{4,0},{8,4},{12,8},{16,12},{20,16},{24,20},{28,24},{1,29},{... | collective-permute-start | bytes 589832 | tf_op jit(solution)/shard_map/ppermute | solution.py:277
  12.8 1.9 %copy-start = (f32[16,3,4,4096]{3,2,1,0:T(4,128)S(1)}, f32[16,3,4,4096]{3,2,1,0:T(4,128)}, u32[]{:S(2)}) copy-start(f32[16,3,4,4096]{3,2,1,0:T(4,128)} %v.7) | copy-start | bytes 9437188
  37.8 9.4 %copy-start.3 = (f32[16]{0:T(128)S(1)}, f32[16]{0:T(128)}, u32[]{:S(2)}) copy-start(f32[16]{0:T(128)} %mx.3) | copy-start | bytes 196

commit v2 on v0

--- a/solution.py
+++ b/solution.py
@@ -16,6 +16,8 @@
 LEADING = 1.0 / (1.0 - 2.0 * ALPHA * RATIO)
 MESH = pl.DeviceIdType.MESH
 TILE = 128
+PARTS = 4
+FIRST = (4, 8)
 
 
 def power(count):
@@ -45,12 +47,12 @@
     return np.concatenate((high, high, low), 0)
 
 
-def edge_weights(cells):
-    away = np.arange(cells, dtype=np.float64)
-    return np.stack((RHO**away, RHO ** (cells - 1 - away))).astype(np.float32)
-
-
-def exchange(nx, ny, v, wy, ein, halo, ygot, vbuf, esend, erecv, ssend, first, last, ysend,
+def signed_power(count):
+    size = jnp.exp(count.astype(jnp.float32) * math.log(RATIO))
+    return jnp.where(count % 2 == 0, size, -size)
+
+
+def exchange(nx, ny, v, ein, halo, ygot, vbuf, esend, erecv, ssend, first, last, ysend,
              load_sem, edge_sem, own_sem, halo_send, halo_recv, e_s, e_r, s_s, s_r, y_s, y_r):
     cells, comps, planes, columns = v.shape
     width = columns // nx
@@ -78,17 +80,22 @@
     pl.semaphore_wait(barrier, nx + ny - 2)
 
     right, left = lax.rem(x + 1, nx), lax.rem(x + nx - 1, nx)
-    rims = [
-        pltpu.make_async_remote_copy(
-            v.at[pl.ds(cells - 2, 2)], halo.at[0], halo_send.at[0], halo_recv.at[0],
-            device_id=(right, y), device_id_type=MESH),
-        pltpu.make_async_remote_copy(
-            v.at[pl.ds(0, 2)], halo.at[1], halo_send.at[1], halo_recv.at[1],
-            device_id=(left, y), device_id_type=MESH),
-    ]
-    for copy in rims:
-        copy.start()
-
+    piece = columns // PARTS
+    rims = []
+    for p in range(PARTS):
+        at = slice(p * piece, (p + 1) * piece)
+        rims += [
+            pltpu.make_async_remote_copy(
+                v.at[cells - 2 :, :, :, at], halo.at[0, :, :, :, at], halo_send.at[2 * p], halo_recv.at[2 * p],
+                device_id=(right, y), device_id_type=MESH),
+            pltpu.make_async_remote_copy(
+                v.at[:2, :, :, at], halo.at[1, :, :, :, at], halo_send.at[2 * p + 1], halo_recv.at[2 * p + 1],
+                device_id=(left, y), device_id_type=MESH),
+        ]
+    cuts = [0, *FIRST, 2 * PARTS]
+    begin = lambda n: [copy.start() for copy in rims[cuts[n] : cuts[n + 1]]]
+
+    begin(0)
     sends = []
     to_low = jnp.zeros((cells, comps, planes, TILE), jnp.float32)
     to_high = jnp.zeros((cells, comps, planes, TILE), jnp.float32)
@@ -113,11 +120,13 @@
             sends.append(copy)
         start = target(q) * width
         for t in range(width // TILE):
-            at = pl.multiple_of(start + t * TILE, TILE)
+            at = start + t * TILE
             part = block[:, :, :, t * TILE : (t + 1) * TILE]
-            for side in range(2):
-                ysum[side] = ysum[side] + part * wy[pl.ds(side, 1), pl.ds(at, TILE)][None, None]
-
+            cell = at + lax.broadcasted_iota(jnp.int32, (1, 1, 1, TILE), 3)
+            for side, away in enumerate((cell, columns - 1 - cell)):
+                ysum[side] = ysum[side] + part * signed_power(away)
+
+    begin(1)
     for copy in edges:
         copy.wait()
     lane = lax.broadcasted_iota(jnp.int32, (cells, comps, planes, TILE), 3)
@@ -157,6 +166,7 @@
         else:
             own_x = pltpu.make_async_copy(ssend.at[q], place, own_sem.at[1])
             own_x.start()
+    begin(2)
     own_y.wait()
     own_x.wait()
     for copy in rims:
@@ -284,7 +294,7 @@
             jax.ShapeDtypeStruct((2, 2, comps, planes, columns), f32),
             jax.ShapeDtypeStruct((ny, cells, comps, planes, TILE), f32),
         ],
-        in_specs=[hbm, pl.BlockSpec(memory_space=pltpu.VMEM)],
+        in_specs=[hbm],
         out_specs=[hbm, hbm, hbm],
         scratch_shapes=[
             pltpu.VMEM((2, cells, comps, planes, width), f32),
@@ -294,13 +304,13 @@
             pltpu.VMEM((cells, comps, planes, TILE), f32),
             pltpu.VMEM((cells, comps, planes, TILE), f32),
             pltpu.VMEM((cells, comps, planes, TILE), f32),
-            dma((2,)), dma((2,)), dma((2,)), dma((2,)), dma((2,)),
+            dma((2,)), dma((2,)), dma((2,)), dma((2 * PARTS,)), dma((2 * PARTS,)),
             dma((nx,)), dma((nx,)), dma((nx,)), dma((nx,)), dma((ny,)), dma((ny,)),
         ],
         compiler_params=pltpu.CompilerParams(
             collective_id=0, has_side_effects=True, vmem_limit_bytes=32 * 2**20),
         name="exchange",
-    )(velocity, edge_weights(columns))
+    )(velocity)
 
     lines = cells * planes
     tiles = columns // TILE

time: 53.5 us -> 49.7 us (0.929)
  Pallas kernels: 48.9 us -> 45.2 us
    pallas_call x1, Pallas kernels: 36.7 us -> 32.9 us  [body(): pl.pallas_call(functools.partial(exchange, nx, ny), out_shape=[jax.ShapeD...]
    unnamed x12 -> x10, local copies, waits for them, and re-layouts: 3.61 us -> 3.57 us
where the time goes in v2:
time: 49.7 us; the launch traced here: 49.4 us
  Pallas kernels  45.2 us (91%)
  local copies, waits for them, and re-layouts  3.57 us (7%)
  between operations  0.68 us (1%)
    pallas_call x1, Pallas kernels, body(): pl.pallas_call(functools.partial(exchange, nx, ny), out_shape=[jax.ShapeD...  32.9 us
    pallas_call x1, Pallas kernels, body(): pl.pallas_call(functools.partial(derive, ny), grid=(comps,), out_shape=[j...  12.3 us
    unnamed x10, local copies, waits for them, and re-layouts  3.57 us

profile of v2, /device:TPU:0, one launch (start us, length us, event | category | flops | bytes accessed | tf_op | source)
XLA Modules:
  0.0 49.4 jit_solution(11567408862350510671)
XLA Ops:
  0.6 0.0 copy-start.4
  0.6 0.0 copy-start
  0.6 1.9 %copy-done = f32[16,3,4,4096]{3,2,1,0:T(4,128)S(1)} copy-done((f32[16,3,4,4096]{3,2,1,0:T(4,128)S(1)}, f32[16,3,4,4096]{3,2,1,0:T(4,128)}, u32[]{:S(2)}) %copy-start) | copy-done | bytes 3145752
  2.5 0.0 copy-start.1
  2.5 32.9 %exchange.1 = (f32[2,3,4,4096]{3,2,1,0:T(4,128)S(1)}, f32[2,2,3,4,4096]{4,3,2,1,0:T(4,128)S(1)}, f32[4,16,3,4,128]{4,3,2,1,0:T(4,128)S(1)}) custom-call(f32[16,3,4,4096]{3,2,1,0:T(4,128)S(1)} %copy-done), custom_call_target="tpu_custom_call" | custom-call | tf_op jit(solution)/shard_map/exchange/pallas_call | solution.py:290
  35.5 0.0 copy-done.4
  35.5 0.0 copy-done.1
  35.5 0.0 copy-start.2
  35.5 1.0 %copy-done.2 = bf16[384,384]{1,0:T(8,128)(2,1)S(1)} copy-done((bf16[384,384]{1,0:T(8,128)(2,1)S(1)}, bf16[384,384]{1,0:T(8,128)(2,1)}, u32[]{:S(2)}) %copy-start.2) | copy-done | bytes 294936
  36.4 0.0 copy-start.3
  36.5 0.7 %copy-done.3 = f32[4096]{0:T(1024)S(1)} copy-done((f32[4096]{0:T(1024)S(1)}, f32[4096]{0:T(1024)}, u32[]{:S(2)}) %copy-start.3) | copy-done | bytes 16408
  37.2 12.3 %derive.1 = (f32[16,3,4,4096]{3,2,1,0:T(4,128)}, f32[16,3,4,4096]{3,2,1,0:T(4,128)}) custom-call(f32[16]{0:T(128)S(1)} %copy-done.4, f32[16,3,4,4096]{3,2,1,0:T(4,128)S(1)} %copy-done.1, f32[2,3,4,4096]{3,2,1,0:T(4,128)S(1)} %get-tuple-element.5.ein, f32[2,2,3,4,4096]{4,3,2,1,0:T(4,128)S(1)} %get-tuple-element.6.halo, ...), custom_call_target="tpu_custom_call" | custom-call | tf_op jit(solution)/shard_map/derive/pallas_call | solution.py:318
Async XLA Ops:
  0.6 34.8 %copy-start.4 = (f32[16]{0:T(128)S(1)}, f32[16]{0:T(128)}, u32[]{:S(2)}) copy-start(f32[16]{0:T(128)} %mx.1) | copy-start | bytes 196
  0.6 1.9 %copy-start = (f32[16,3,4,4096]{3,2,1,0:T(4,128)S(1)}, f32[16,3,4,4096]{3,2,1,0:T(4,128)}, u32[]{:S(2)}) copy-start(f32[16,3,4,4096]{3,2,1,0:T(4,128)} %v.3) | copy-start | bytes 9437188
  2.5 32.9 %copy-start.1 = (f32[16,3,4,4096]{3,2,1,0:T(4,128)S(1)}, f32[16,3,4,4096]{3,2,1,0:T(4,128)}, u32[]{:S(2)}) copy-start(f32[16,3,4,4096]{3,2,1,0:T(4,128)} %v.3) | copy-start | bytes 9437188
  35.5 1.0 %copy-start.2 = (bf16[384,384]{1,0:T(8,128)(2,1)S(1)}, bf16[384,384]{1,0:T(8,128)(2,1)}, u32[]{:S(2)}) copy-start(bf16[384,384]{1,0:T(8,128)(2,1)} %constant.2.clone.table) | copy-start | bytes 884740
  36.4 0.7 %copy-start.3 = (f32[4096]{0:T(1024)S(1)}, f32[4096]{0:T(1024)}, u32[]{:S(2)}) copy-start(f32[4096]{0:T(1024)} %param.6) | copy-start | bytes 49156
